TPU v7x, 32 devices: a whole 2x2x4 slice. The times are simulated.
32 devices in a mesh: bits: 8 (over z, core), cuts: 4 (over y, x).
Axes of the slice: x: 2, y: 2, z: 4, core: 2. Of those that a mesh axis runs over, the one named last changes fastest.
Arguments:
- boundary: float32 [4, 16384, 128], P('cuts', 'bits'), may hold values from -6 to 6
- gate_stack: float32 [34, 128, 128], replicated, may hold values from -0.5 to 0.5
- coupling: float32 [13, 128, 128], replicated, may hold values from 0.4 to 1.6
Outputs:
- probs: float32 [16384, 128], P('bits', 'cuts')
All inputs are finite; a program needn't handle non-finite values.
Results may differ from a plain program's by a relative error of at most 0.00018.
Values sent between devices are 32-bit elements; how exact they have to be, the bound alone decides.
A program may use at most 64 MiB of HBM per device.

v0:
```python
import functools

import jax
import jax.numpy as jnp
from jax import lax
from jax.experimental import pallas as pl
from jax.experimental.pallas import tpu as pltpu
from jax.sharding import PartitionSpec as P

MESH = pl.DeviceIdType.MESH
CYC_A = 4
CYC_B = 4
CYC_C = 5
G = 128
F32 = jnp.float32
BF16 = jnp.bfloat16


def split(x):
    hi = x.astype(BF16)
    lo = (x - hi.astype(F32)).astype(BF16)
    return hi, lo


def left_gate(w_ref, index, x):
    hi, lo = w_ref[index, 0], w_ref[index, 1]
    lhs = jnp.concatenate([jnp.concatenate([hi, hi], 1), jnp.concatenate([lo, lo], 1)], 0)
    xh, xl = split(x)
    y = jnp.dot(lhs, jnp.concatenate([xh, xl], 0), preferred_element_type=F32)
    return y[:G] + y[G:]


def right_gate(w_ref, index, x):
    row = jnp.concatenate([w_ref[index, 0], w_ref[index, 1]], 1)
    rhs = jnp.concatenate([row, row], 0)
    xh, xl = split(x)
    y = jnp.dot(jnp.concatenate([xh, xl], 1), rhs, preferred_element_type=F32)
    return y[:, :G] + y[:, G:]


def lane_blocks(shape, width):
    return lax.broadcasted_iota(jnp.int32, shape, 1) // width


def transpose_blocks(parts, width):
    n = len(parts)
    parts = list(parts)
    block = lane_blocks(parts[0].shape, width)
    m = 1
    while m < n:
        zero = (block // m) % 2 == 0
        for g in range(n):
            if g & m == 0:
                lo, hi = parts[g], parts[g | m]
                parts[g] = jnp.where(zero, lo, pltpu.roll(hi, m * width, 1))
                parts[g | m] = jnp.where(zero, pltpu.roll(lo, G - m * width, 1), hi)
        m *= 2
    return parts


def repack(src, dst, n, width):
    groups = 16 // n
    for p in range(groups):
        for q in range(groups):
            parts = transpose_blocks([src[p, q * n + h] for h in range(n)], width)
            for g in range(n):
                dst[q, p * n + g] = parts[g]


def kernel(
    n, nb, x_hbm, gate_ref, cpl_ref, out_ref,
    x, wt, wl, wm, tab, tmp, rs_buf, red, swp, sbuf, rbuf, mp, tp, in0,
    rs_send, rs_recv, swp_sem, fin_send, fin_recv, in0_sem,
):
    me = lax.axis_index("cuts")
    bit = lax.axis_index("bits")
    width = G // n
    groups = 16 // n
    top_mask = nb // 2
    par_top = (bit // top_mask) % 2
    par_low = bit % 2
    mate_top = bit + (1 - 2 * par_top) * top_mask
    mate_low = bit + 1 - 2 * par_low
    out_base = (1 - par_top) * 8
    stay_base = par_top * 8

    barrier = pltpu.get_barrier_semaphore()
    for d in range(1, n):
        pl.semaphore_signal(barrier, inc=1, device_id=(bit, lax.rem(me + d, n)), device_id_type=MESH)
    pl.semaphore_signal(barrier, inc=1, device_id=(mate_top, me), device_id_type=MESH)
    pl.semaphore_signal(barrier, inc=1, device_id=(mate_low, me), device_id_type=MESH)

    def share(ref, base, k):
        if n <= 8:
            return ref.at[pl.ds(base + k * (8 // n), 8 // n)]
        cut = n // 8
        return ref.at[base + k // cut, pl.ds((k % cut) * (16 // cut), 16 // cut)]

    eye = jnp.where(
        lax.broadcasted_iota(jnp.int32, (G, G), 0) == lax.broadcasted_iota(jnp.int32, (G, G), 1), F32(0.9), F32(0.0)
    )

    def put(w_ref, index, value):
        hi, lo = split(value)
        w_ref[index, 0] = hi
        w_ref[index, 1] = lo

    def reorder(load):
        return jnp.concatenate([load(c) for c in range(16)], 0)

    def prep_top(index, gate):
        put(wt, index, (eye + 0.45 * gate_ref[gate]).T)

    def prep_lane(index, gate):
        put(wl, index, eye + 0.45 * gate_ref[gate])

    def prep_mid(index, gate, natural=False):
        rows = reorder(lambda c: gate_ref[gate, pl.ds(c, 8, stride=16), :])
        if natural:
            diag = tmp_eye()
            put(wm, index, diag + 0.45 * rows.T)
        else:
            tmp[...] = rows.T
            put(wm, index, eye + 0.45 * reorder(lambda c: tmp[pl.ds(c, 8, stride=16), :]))

    def tmp_eye():
        r = lax.broadcasted_iota(jnp.int32, (G, G), 0)
        c = lax.broadcasted_iota(jnp.int32, (G, G), 1)
        return jnp.where((c % 8) * 16 + c // 8 == r, F32(0.9), F32(0.0))

    def prep_table(index, packed):
        value = reorder(lambda c: cpl_ref[index, pl.ds(c, 8, stride=16), :])
        if packed:
            value = jnp.where(lane_blocks((G, G), width) == me, value, 0.0)
            m = 1
            while m < n:
                value = value + pltpu.roll(value, m * width, 1)
                m *= 2
        tab[index] = value

    def prep_layers(first, count):
        @pl.loop(first, first + count)
        def _(layer):
            prep_top(layer, 3 * layer)
            prep_lane(layer, 3 * layer + 1)
            prep_mid(layer, 3 * layer + 2)

    def top(layer):
        for j in range(8):
            pair = [x[:, 2 * j + u].reshape(G, G) for u in range(2)]
            y = left_gate(wt, layer, jnp.concatenate(pair, 1))
            for u in range(2):
                x[:, 2 * j + u] = y[:, u * G:(u + 1) * G].reshape(16, 8, G)

    def lane_mid(layer, base, count):
        for j in range(0, count, 4):
            y = right_gate(wl, layer, x[pl.ds(base + j, 4)].reshape(4 * G, G))
            table = tab[layer]
            y = jnp.concatenate([y[u * G:(u + 1) * G] * table for u in range(4)], 1)
            y = left_gate(wm, layer, y)
            for u in range(4):
                x[base + j + u] = y[:, u * G:(u + 1) * G].reshape(16, 8, G)

    prep_layers(0, CYC_A)

    @pl.loop(0, CYC_A)
    def _(layer):
        prep_table(layer, False)

    for t in range(16):
        x[:, t] = x_hbm[pl.ds(t, G, stride=16), :].reshape(16, 8, G)

    @pl.loop(0, CYC_A - 1)
    def _(layer):
        top(layer)
        lane_mid(layer, 0, 16)

    top(CYC_A - 1)
    lane_mid(CYC_A - 1, out_base, 8)

    pl.semaphore_wait(barrier, n + 1)
    rs = []
    for d in range(1, n):
        to = lax.rem(me + d, n)
        rs.append(pltpu.make_async_remote_copy(
            src_ref=share(x, out_base, to), dst_ref=rs_buf.at[d - 1],
            send_sem=rs_send.at[d - 1], recv_sem=rs_recv.at[d - 1],
            device_id=(bit, to), device_id_type=MESH,
        ))
        rs[-1].start()
    lane_mid(CYC_A - 1, stay_base, 8)
    prep_layers(CYC_A, CYC_B)

    @pl.loop(CYC_A, CYC_A + CYC_B - 1)
    def _(layer):
        prep_table(layer, False)

    for copy in rs:
        copy.wait_recv()
    total = share(x, out_base, me)[...]
    for d in range(1, n):
        total = total + rs_buf[d - 1]
    red[...] = total
    swap = pltpu.make_async_remote_copy(
        src_ref=red, dst_ref=swp, send_sem=swp_sem.at[0], recv_sem=swp_sem.at[1],
        device_id=(mate_top, me), device_id_type=MESH,
    )
    swap.start()

    @pl.loop(CYC_A + CYC_B - 1, CYC_A + CYC_B + CYC_C)
    def _(layer):
        prep_table(layer, True)

    last = CYC_A + CYC_B
    @pl.loop(0, CYC_C)
    def _(turn):
        prep_top(last + turn, 3 * last + 2 * turn)

    @pl.loop(0, CYC_C - 1)
    def _(turn):
        prep_mid(last + turn, 3 * last + 2 * turn + 1)

    prep_mid(last + CYC_C - 1, 3 * last + 2 * (CYC_C - 1) + 1, natural=True)

    for copy in rs:
        copy.wait_send()
    for j in range(8):
        x[out_base + j] = jnp.zeros((16, 8, G), F32)
    swap.wait()
    share(x, out_base, me)[...] = swp[...]

    @pl.loop(CYC_A, CYC_A + CYC_B - 1)
    def _(layer):
        top(layer)
        lane_mid(layer, 0, 16)

    final = CYC_A + CYC_B - 1
    top(final)
    for p in range(groups):
        y = right_gate(wl, final, x[pl.ds(p * n, n)].reshape(n * G, G))
        parts = transpose_blocks([y[g * G:(g + 1) * G] for g in range(n)], width)
        for k in range(n):
            sbuf[k, p] = parts[k].reshape(16, 8, G)

    fin = []
    for d in range(1, n):
        to = lax.rem(me + d, n)
        fin.append(pltpu.make_async_remote_copy(
            src_ref=sbuf.at[to], dst_ref=rbuf.at[d - 1],
            send_sem=fin_send.at[d - 1], recv_sem=fin_recv.at[d - 1],
            device_id=(bit, to), device_id_type=MESH,
        ))
        fin[-1].start()
    for copy in fin:
        copy.wait_recv()

    def mid_packed(layer, load):
        table = tab[layer]
        y = jnp.concatenate([load(p) * table for p in range(groups)], 1)
        return left_gate(wm, layer, y)

    def load_sum(p):
        total = sbuf[me, p]
        for d in range(1, n):
            total = total + rbuf[d - 1, p]
        return total.reshape(G, G)

    def put_packed(ref, y):
        for p in range(groups):
            ref[p] = y[:, p * G:(p + 1) * G].reshape(16, 8, G)

    put_packed(mp, mid_packed(final, load_sum))
    repack(mp, tp, n, width)

    swap_low = pltpu.make_async_remote_copy(
        src_ref=tp.at[:, pl.ds((1 - par_low) * 8, 8)], dst_ref=in0,
        send_sem=in0_sem.at[0], recv_sem=in0_sem.at[1],
        device_id=(mate_low, me), device_id_type=MESH,
    )
    swap_low.start()
    for copy in fin:
        copy.wait_send()
    swap_low.wait()
    tp[:, pl.ds((1 - par_low) * 8, 8)] = in0[...]

    def top_packed(layer):
        y = jnp.concatenate([tp[p].reshape(G, G) for p in range(groups)], 1)
        put_packed(tp, left_gate(wt, layer, y))
        repack(tp, mp, n, width)

    @pl.loop(last, last + CYC_C - 1)
    def _(layer):
        top_packed(layer)
        put_packed(mp, mid_packed(layer, lambda p: mp[p].reshape(G, G)))
        repack(mp, tp, n, width)

    end = last + CYC_C - 1
    top_packed(end)
    y = mid_packed(end, lambda p: mp[p].reshape(G, G))
    for p in range(groups):
        part = y[:, p * G:(p + 1) * G]
        for g in range(n):
            moved = part if g == 0 else pltpu.roll(part, G - g * width, 1)
            out_ref[pl.ds((p * n + g) * G, G), :] = moved[:, :width]


def solution(mesh):
    n, nb = mesh.shape["cuts"], mesh.shape["bits"]
    groups = 16 // n
    part = (8 // n, 16, 8, G) if n <= 8 else (16 // (n // 8), 8, G)

    def on_device(boundary, gate_stack, coupling):
        vmem = pl.BlockSpec(memory_space=pltpu.VMEM)
        layers = CYC_A + CYC_B + CYC_C
        return pl.pallas_call(
            functools.partial(kernel, n, nb),
            out_shape=jax.ShapeDtypeStruct((boundary.shape[1], G // n), F32),
            in_specs=[vmem] * 3,
            out_specs=vmem,
            scratch_shapes=[
                pltpu.VMEM((16, 16, 8, G), F32),
                pltpu.VMEM((layers, 2, G, G), BF16),
                pltpu.VMEM((CYC_A + CYC_B, 2, G, G), BF16),
                pltpu.VMEM((layers, 2, G, G), BF16),
                pltpu.VMEM((layers, G, G), F32),
                pltpu.VMEM((G, G), F32),
                pltpu.VMEM((n - 1,) + part, F32),
                pltpu.VMEM(part, F32),
                pltpu.VMEM(part, F32),
                pltpu.VMEM((n, groups, 16, 8, G), F32),
                pltpu.VMEM((n - 1, groups, 16, 8, G), F32),
                pltpu.VMEM((groups, 16, 8, G), F32),
                pltpu.VMEM((groups, 16, 8, G), F32),
                pltpu.VMEM((groups, 8, 8, G), F32),
                pltpu.SemaphoreType.DMA((n - 1,)),
                pltpu.SemaphoreType.DMA((n - 1,)),
                pltpu.SemaphoreType.DMA((2,)),
                pltpu.SemaphoreType.DMA((n - 1,)),
                pltpu.SemaphoreType.DMA((n - 1,)),
                pltpu.SemaphoreType.DMA((2,)),
            ],
            compiler_params=pltpu.CompilerParams(
                collective_id=0, has_side_effects=True, vmem_limit_bytes=40 * 2**20
            ),
        )(boundary[0], gate_stack, coupling)

    return jax.shard_map(
        on_device, mesh=mesh, in_specs=(P("cuts", "bits", None), P(), P()), out_specs=P("bits", "cuts"), check_vma=False
    )
```

profile of v0, /device:TPU:0, one launch (start us, length us, event | category | flops | bytes accessed | tf_op | source)
XLA Modules:
  0.0 51.5 jit_solution(178481352094374059)
XLA Ops:
  0.0 0.0 copy-start
  0.0 1.6 %copy-done = f32[34,128,128]{2,1,0:T(8,128)S(1)} copy-done((f32[34,128,128]{2,1,0:T(8,128)S(1)}, f32[34,128,128]{2,1,0:T(8,128)}, u32[]{:S(2)}) %copy-start) | copy-done | bytes 2228248
  1.6 0.0 copy-start.1
  1.6 1.2 %copy-done.1 = f32[1,2048,128]{2,1,0:T(8,128)S(1)} copy-done((f32[1,2048,128]{2,1,0:T(8,128)S(1)}, f32[1,2048,128]{2,1,0:T(8,128)}, u32[]{:S(2)}) %copy-start.1) | copy-done | bytes 1048600
  2.9 0.0 copy-start.2
  2.9 1.2 %copy-done.2 = f32[13,128,128]{2,1,0:T(8,128)S(1)} copy-done((f32[13,128,128]{2,1,0:T(8,128)S(1)}, f32[13,128,128]{2,1,0:T(8,128)}, u32[]{:S(2)}) %copy-start.2) | copy-done | bytes 851992
  4.0 46.5 %shard_map.37 = f32[2048,32]{1,0:T(8,128)S(1)} custom-call(f32[2048,128]{1,0:T(8,128)S(1)} %bitcast.1, f32[34,128,128]{2,1,0:T(8,128)S(1)} %copy-done, f32[13,128,128]{2,1,0:T(8,128)S(1)} %copy-done.2), custom_call_target="tpu_custom_call" | custom-call | tf_op jit(solution)/shard_map/pallas_call | solution.py:315
  50.5 1.0 %copy.4 = f32[2048,32]{0,1:T(8,128)} copy(f32[2048,32]{1,0:T(8,128)S(1)} %shard_map.37) | data formatting | bytes 524288 | tf_op jit(solution)/shard_map/pallas_call | solution.py:315
Async XLA Ops:
  0.0 1.6 %copy-start = (f32[34,128,128]{2,1,0:T(8,128)S(1)}, f32[34,128,128]{2,1,0:T(8,128)}, u32[]{:S(2)}) copy-start(f32[34,128,128]{2,1,0:T(8,128)} %gate_ref.1) | copy-start | bytes 6684676
  1.6 1.2 %copy-start.1 = (f32[1,2048,128]{2,1,0:T(8,128)S(1)}, f32[1,2048,128]{2,1,0:T(8,128)}, u32[]{:S(2)}) copy-start(f32[1,2048,128]{2,1,0:T(8,128)} %param.3) | copy-start | bytes 3145732
  2.9 1.2 %copy-start.2 = (f32[13,128,128]{2,1,0:T(8,128)S(1)}, f32[13,128,128]{2,1,0:T(8,128)}, u32[]{:S(2)}) copy-start(f32[13,128,128]{2,1,0:T(8,128)} %cpl_ref.1) | copy-start | bytes 2555908
where the time goes:
time: 51.8 us; the launch traced here: 51.5 us
  Pallas kernels  46.5 us (90%)
  local copies, waits for them, and re-layouts  5.02 us (10%)
    pallas_call x1, Pallas kernels, on_device(): pl.pallas_call(functools.partial(kernel, n, nb), out_shape=jax.ShapeDtype...  46.5 us
    unnamed x6, local copies, waits for them, and re-layouts  4.01 us

commit v1 on v0

--- a/solution.py
+++ b/solution.py
@@ -68,10 +68,23 @@
 
 
 def kernel(
-    n, nb, x_hbm, gate_ref, cpl_ref, out_ref,
-    x, wt, wl, wm, tab, tmp, rs_buf, red, swp, sbuf, rbuf, mp, tp, in0,
-    rs_send, rs_recv, swp_sem, fin_send, fin_recv, in0_sem,
+    n, nb, x_hbm, gate_hbm, cpl_hbm, out_ref,
+    x_in, gate_ref, cpl_ref, x, wt, wl, wm, tab, tmp, rs_buf, red, swp, sbuf, rbuf, mp, tp, in0,
+    in_sem, rs_send, rs_recv, swp_send, swp_recv, fin_send, fin_recv, in0_sem,
 ):
+    spans = ((0, 3), (3, 3 * CYC_A), (3 * CYC_A, gate_ref.shape[0]))
+    loads = [
+        pltpu.make_async_copy(gate_hbm.at[pl.ds(a, b - a)], gate_ref.at[pl.ds(a, b - a)], in_sem.at[i])
+        for i, (a, b) in enumerate(spans)
+    ]
+    load_cpl = pltpu.make_async_copy(cpl_hbm, cpl_ref, in_sem.at[3])
+    load_x = pltpu.make_async_copy(x_hbm.at[0], x_in, in_sem.at[4])
+    loads[0].start()
+    load_x.start()
+    load_cpl.start()
+    loads[1].start()
+    loads[2].start()
+
     me = lax.axis_index("cuts")
     bit = lax.axis_index("bits")
     width = G // n
@@ -90,9 +103,11 @@
     pl.semaphore_signal(barrier, inc=1, device_id=(mate_top, me), device_id_type=MESH)
     pl.semaphore_signal(barrier, inc=1, device_id=(mate_low, me), device_id_type=MESH)
 
-    def share(ref, base, k):
+    rounds = max(8 // n, 1)
+
+    def share(ref, base, k, r):
         if n <= 8:
-            return ref.at[pl.ds(base + k * (8 // n), 8 // n)]
+            return ref.at[base + k * rounds + r]
         cut = n // 8
         return ref.at[base + k // cut, pl.ds((k % cut) * (16 // cut), 16 // cut)]
 
@@ -138,12 +153,13 @@
                 m *= 2
         tab[index] = value
 
+    def prep_layer(layer):
+        prep_top(layer, 3 * layer)
+        prep_lane(layer, 3 * layer + 1)
+        prep_mid(layer, 3 * layer + 2)
+
     def prep_layers(first, count):
-        @pl.loop(first, first + count)
-        def _(layer):
-            prep_top(layer, 3 * layer)
-            prep_lane(layer, 3 * layer + 1)
-            prep_mid(layer, 3 * layer + 2)
+        pl.loop(first, first + count)(prep_layer)
 
     def top(layer):
         for j in range(8):
@@ -152,60 +168,72 @@
             for u in range(2):
                 x[:, 2 * j + u] = y[:, u * G:(u + 1) * G].reshape(16, 8, G)
 
-    def lane_mid(layer, base, count):
-        for j in range(0, count, 4):
-            y = right_gate(wl, layer, x[pl.ds(base + j, 4)].reshape(4 * G, G))
+    def lane_mid(layer, blocks):
+        for j in range(0, len(blocks), 4):
+            y = right_gate(wl, layer, jnp.concatenate([x[blocks[j + u]].reshape(G, G) for u in range(4)], 0))
             table = tab[layer]
             y = jnp.concatenate([y[u * G:(u + 1) * G] * table for u in range(4)], 1)
             y = left_gate(wm, layer, y)
             for u in range(4):
-                x[base + j + u] = y[:, u * G:(u + 1) * G].reshape(16, 8, G)
-
-    prep_layers(0, CYC_A)
-
-    @pl.loop(0, CYC_A)
-    def _(layer):
-        prep_table(layer, False)
-
+                x[blocks[j + u]] = y[:, u * G:(u + 1) * G].reshape(16, 8, G)
+
+    loads[0].wait()
+    prep_layers(0, 1)
+    load_cpl.wait()
+    prep_table(0, False)
+    load_x.wait()
     for t in range(16):
-        x[:, t] = x_hbm[pl.ds(t, G, stride=16), :].reshape(16, 8, G)
+        x[:, t] = x_in[pl.ds(t, G, stride=16), :].reshape(16, 8, G)
+    loads[1].wait()
 
     @pl.loop(0, CYC_A - 1)
     def _(layer):
         top(layer)
-        lane_mid(layer, 0, 16)
+        lane_mid(layer, range(16))
+        prep_layer(layer + 1)
+        prep_table(layer + 1, False)
 
     top(CYC_A - 1)
-    lane_mid(CYC_A - 1, out_base, 8)
-
-    pl.semaphore_wait(barrier, n + 1)
+
     rs = []
-    for d in range(1, n):
-        to = lax.rem(me + d, n)
-        rs.append(pltpu.make_async_remote_copy(
-            src_ref=share(x, out_base, to), dst_ref=rs_buf.at[d - 1],
-            send_sem=rs_send.at[d - 1], recv_sem=rs_recv.at[d - 1],
-            device_id=(bit, to), device_id_type=MESH,
+    for r in range(rounds):
+        if rounds == 2:
+            lane_mid(CYC_A - 1, [out_base + 2 * i + r for i in range(4)])
+        elif r == 0:
+            lane_mid(CYC_A - 1, [out_base + i for i in range(8)])
+        if r == 0:
+            pl.semaphore_wait(barrier, n + 1)
+        rs.append([])
+        for d in range(1, n):
+            to = lax.rem(me + d, n)
+            rs[r].append(pltpu.make_async_remote_copy(
+                src_ref=share(x, out_base, to, r), dst_ref=rs_buf.at[r, d - 1],
+                send_sem=rs_send.at[r, d - 1], recv_sem=rs_recv.at[r, d - 1],
+                device_id=(bit, to), device_id_type=MESH,
+            ))
+            rs[r][-1].start()
+    lane_mid(CYC_A - 1, [stay_base + i for i in range(8)])
+    loads[2].wait()
+
+    swaps = []
+    for r in range(rounds):
+        for copy in rs[r]:
+            copy.wait_recv()
+        total = share(x, out_base, me, r)[...]
+        for d in range(1, n):
+            total = total + rs_buf[r, d - 1]
+        red[r] = total
+        swaps.append(pltpu.make_async_remote_copy(
+            src_ref=red.at[r], dst_ref=swp.at[r], send_sem=swp_send.at[r], recv_sem=swp_recv.at[r],
+            device_id=(mate_top, me), device_id_type=MESH,
         ))
-        rs[-1].start()
-    lane_mid(CYC_A - 1, stay_base, 8)
+        swaps[r].start()
+
     prep_layers(CYC_A, CYC_B)
 
     @pl.loop(CYC_A, CYC_A + CYC_B - 1)
     def _(layer):
         prep_table(layer, False)
-
-    for copy in rs:
-        copy.wait_recv()
-    total = share(x, out_base, me)[...]
-    for d in range(1, n):
-        total = total + rs_buf[d - 1]
-    red[...] = total
-    swap = pltpu.make_async_remote_copy(
-        src_ref=red, dst_ref=swp, send_sem=swp_sem.at[0], recv_sem=swp_sem.at[1],
-        device_id=(mate_top, me), device_id_type=MESH,
-    )
-    swap.start()
 
     @pl.loop(CYC_A + CYC_B - 1, CYC_A + CYC_B + CYC_C)
     def _(layer):
@@ -222,17 +250,19 @@
 
     prep_mid(last + CYC_C - 1, 3 * last + 2 * (CYC_C - 1) + 1, natural=True)
 
-    for copy in rs:
-        copy.wait_send()
+    for r in range(rounds):
+        for copy in rs[r]:
+            copy.wait_send()
     for j in range(8):
         x[out_base + j] = jnp.zeros((16, 8, G), F32)
-    swap.wait()
-    share(x, out_base, me)[...] = swp[...]
+    for r in range(rounds):
+        swaps[r].wait()
+        share(x, out_base, me, r)[...] = swp[r]
 
     @pl.loop(CYC_A, CYC_A + CYC_B - 1)
     def _(layer):
         top(layer)
-        lane_mid(layer, 0, 16)
+        lane_mid(layer, range(16))
 
     final = CYC_A + CYC_B - 1
     top(final)
@@ -242,17 +272,37 @@
         for k in range(n):
             sbuf[k, p] = parts[k].reshape(16, 8, G)
 
+    def send(src, dst, index, to):
+        copy = pltpu.make_async_remote_copy(
+            src_ref=src, dst_ref=dst, send_sem=fin_send.at[index], recv_sem=fin_recv.at[index],
+            device_id=(bit, to), device_id_type=MESH,
+        )
+        copy.start()
+        return copy
+
     fin = []
-    for d in range(1, n):
-        to = lax.rem(me + d, n)
-        fin.append(pltpu.make_async_remote_copy(
-            src_ref=sbuf.at[to], dst_ref=rbuf.at[d - 1],
-            send_sem=fin_send.at[d - 1], recv_sem=fin_recv.at[d - 1],
-            device_id=(bit, to), device_id_type=MESH,
-        ))
-        fin[-1].start()
-    for copy in fin:
-        copy.wait_recv()
+    if n == 4:
+        near = (me + 1 - 2 * (me % 2), me + 2 - 4 * (me // 2))
+        far = 3 - me
+        first = [send(sbuf.at[far, p], rbuf.at[0, p], p, near[p % 2]) for p in range(groups)]
+        second = [send(sbuf.at[near[p % 2], p], rbuf.at[1, p], groups + p, near[p % 2]) for p in range(groups)]
+        third = []
+        for p in range(groups):
+            first[p].wait_recv()
+            to = near[1 - p % 2]
+            sbuf[to, p] = sbuf[to, p] + rbuf[0, p]
+            third.append(send(sbuf.at[to, p], rbuf.at[2, p], 2 * groups + p, to))
+        for copy in second + third:
+            copy.wait_recv()
+        fin = first + second + third
+        terms = (1, 2)
+    else:
+        for d in range(1, n):
+            to = lax.rem(me + d, n)
+            fin.append(send(sbuf.at[to], rbuf.at[d - 1], d - 1, to))
+        for copy in fin:
+            copy.wait_recv()
+        terms = range(n - 1)
 
     def mid_packed(layer, load):
         table = tab[layer]
@@ -261,8 +311,8 @@
 
     def load_sum(p):
         total = sbuf[me, p]
-        for d in range(1, n):
-            total = total + rbuf[d - 1, p]
+        for d in terms:
+            total = total + rbuf[d, p]
         return total.reshape(G, G)
 
     def put_packed(ref, y):
@@ -307,24 +357,29 @@
 def solution(mesh):
     n, nb = mesh.shape["cuts"], mesh.shape["bits"]
     groups = 16 // n
-    part = (8 // n, 16, 8, G) if n <= 8 else (16 // (n // 8), 8, G)
+    rounds = max(8 // n, 1)
+    part = (rounds, 16 // max(n // 8, 1), 8, G)
+    messages = 3 * groups if n == 4 else n - 1
 
     def on_device(boundary, gate_stack, coupling):
-        vmem = pl.BlockSpec(memory_space=pltpu.VMEM)
+        gates, tables = gate_stack.shape[0], coupling.shape[0]
         layers = CYC_A + CYC_B + CYC_C
         return pl.pallas_call(
             functools.partial(kernel, n, nb),
             out_shape=jax.ShapeDtypeStruct((boundary.shape[1], G // n), F32),
-            in_specs=[vmem] * 3,
-            out_specs=vmem,
+            in_specs=[pl.BlockSpec(memory_space=pltpu.HBM)] * 3,
+            out_specs=pl.BlockSpec(memory_space=pltpu.VMEM),
             scratch_shapes=[
+                pltpu.VMEM(boundary.shape[1:], F32),
+                pltpu.VMEM((gates, G, G), F32),
+                pltpu.VMEM((tables, G, G), F32),
                 pltpu.VMEM((16, 16, 8, G), F32),
                 pltpu.VMEM((layers, 2, G, G), BF16),
                 pltpu.VMEM((CYC_A + CYC_B, 2, G, G), BF16),
                 pltpu.VMEM((layers, 2, G, G), BF16),
                 pltpu.VMEM((layers, G, G), F32),
                 pltpu.VMEM((G, G), F32),
-                pltpu.VMEM((n - 1,) + part, F32),
+                pltpu.VMEM((rounds, n - 1) + part[1:], F32),
                 pltpu.VMEM(part, F32),
                 pltpu.VMEM(part, F32),
                 pltpu.VMEM((n, groups, 16, 8, G), F32),
@@ -332,17 +387,19 @@
                 pltpu.VMEM((groups, 16, 8, G), F32),
                 pltpu.VMEM((groups, 16, 8, G), F32),
                 pltpu.VMEM((groups, 8, 8, G), F32),
-                pltpu.SemaphoreType.DMA((n - 1,)),
-                pltpu.SemaphoreType.DMA((n - 1,)),
-                pltpu.SemaphoreType.DMA((2,)),
-                pltpu.SemaphoreType.DMA((n - 1,)),
-                pltpu.SemaphoreType.DMA((n - 1,)),
+                pltpu.SemaphoreType.DMA((5,)),
+                pltpu.SemaphoreType.DMA((rounds, n - 1)),
+                pltpu.SemaphoreType.DMA((rounds, n - 1)),
+                pltpu.SemaphoreType.DMA((rounds,)),
+                pltpu.SemaphoreType.DMA((rounds,)),
+                pltpu.SemaphoreType.DMA((messages,)),
+                pltpu.SemaphoreType.DMA((messages,)),
                 pltpu.SemaphoreType.DMA((2,)),
             ],
             compiler_params=pltpu.CompilerParams(
                 collective_id=0, has_side_effects=True, vmem_limit_bytes=40 * 2**20
             ),
-        )(boundary[0], gate_stack, coupling)
+        )(boundary, gate_stack, coupling)
 
     return jax.shard_map(
         on_device, mesh=mesh, in_specs=(P("cuts", "bits", None), P(), P()), out_specs=P("bits", "cuts"), check_vma=False

time: 51.8 us -> 48.2 us (0.931)
  Pallas kernels: 46.5 us -> 43 us
    pallas_call x1, Pallas kernels: 46.5 us -> 43 us  [on_device(): pl.pallas_call(functools.partial(kernel, n, nb), out_shape=jax.ShapeDtype...]
where the time goes in v1:
time: 48.2 us; the launch traced here: 48 us
  Pallas kernels  43 us (89%)
  local copies, waits for them, and re-layouts  5.02 us (10%)
    pallas_call x1, Pallas kernels, on_device(): pl.pallas_call(functools.partial(kernel, n, nb), out_shape=jax.ShapeDtype...  43 us
    unnamed x6, local copies, waits for them, and re-layouts  4.01 us
    pallas_call x1, local copies, waits for them, and re-layouts, on_device(): pl.pallas_call(functools.partial(kernel, n, nb), out_shape=jax.ShapeDtype...  1.01 us

profile of v1, /device:TPU:0, one launch (start us, length us, event | category | flops | bytes accessed | tf_op | source)
XLA Modules:
  0.0 48.0 jit_solution(14735327037114579787)
XLA Ops:
  0.0 0.0 copy-start
  0.0 1.6 %copy-done = f32[34,128,128]{2,1,0:T(8,128)S(1)} copy-done((f32[34,128,128]{2,1,0:T(8,128)S(1)}, f32[34,128,128]{2,1,0:T(8,128)}, u32[]{:S(2)}) %copy-start) | copy-done | bytes 2228248
  1.6 0.0 copy-start.1
  1.6 1.2 %copy-done.1 = f32[1,2048,128]{2,1,0:T(8,128)S(1)} copy-done((f32[1,2048,128]{2,1,0:T(8,128)S(1)}, f32[1,2048,128]{2,1,0:T(8,128)}, u32[]{:S(2)}) %copy-start.1) | copy-done | bytes 1048600
  2.9 0.0 copy-start.2
  2.9 1.2 %copy-done.2 = f32[13,128,128]{2,1,0:T(8,128)S(1)} copy-done((f32[13,128,128]{2,1,0:T(8,128)S(1)}, f32[13,128,128]{2,1,0:T(8,128)}, u32[]{:S(2)}) %copy-start.2) | copy-done | bytes 851992
  4.0 43.0 %shard_map.37 = f32[2048,32]{1,0:T(8,128)S(1)} custom-call(f32[1,2048,128]{2,1,0:T(8,128)S(1)} %copy-done.1, f32[34,128,128]{2,1,0:T(8,128)S(1)} %copy-done, f32[13,128,128]{2,1,0:T(8,128)S(1)} %copy-done.2), custom_call_target="tpu_custom_call" | custom-call | tf_op jit(solution)/shard_map/pallas_call | solution.py:367
  47.0 1.0 %copy.4 = f32[2048,32]{0,1:T(8,128)} copy(f32[2048,32]{1,0:T(8,128)S(1)} %shard_map.37) | data formatting | bytes 524288 | tf_op jit(solution)/shard_map/pallas_call | solution.py:367
Async XLA Ops:
  0.0 1.6 %copy-start = (f32[34,128,128]{2,1,0:T(8,128)S(1)}, f32[34,128,128]{2,1,0:T(8,128)}, u32[]{:S(2)}) copy-start(f32[34,128,128]{2,1,0:T(8,128)} %gate_hbm.1) | copy-start | bytes 6684676
  1.6 1.2 %copy-start.1 = (f32[1,2048,128]{2,1,0:T(8,128)S(1)}, f32[1,2048,128]{2,1,0:T(8,128)}, u32[]{:S(2)}) copy-start(f32[1,2048,128]{2,1,0:T(8,128)} %x_hbm.1) | copy-start | bytes 3145732
  2.9 1.2 %copy-start.2 = (f32[13,128,128]{2,1,0:T(8,128)S(1)}, f32[13,128,128]{2,1,0:T(8,128)}, u32[]{:S(2)}) copy-start(f32[13,128,128]{2,1,0:T(8,128)} %cpl_hbm.1) | copy-start | bytes 2555908

commit v2 on v1

--- a/solution.py
+++ b/solution.py
@@ -14,6 +14,7 @@
 G = 128
 F32 = jnp.float32
 BF16 = jnp.bfloat16
+VMEM_BYTES = 63 * 2**20 + 2**19
 
 
 def split(x):
@@ -349,9 +350,9 @@
     y = mid_packed(end, lambda p: mp[p].reshape(G, G))
     for p in range(groups):
         part = y[:, p * G:(p + 1) * G]
+        part = part.T
         for g in range(n):
-            moved = part if g == 0 else pltpu.roll(part, G - g * width, 1)
-            out_ref[pl.ds((p * n + g) * G, G), :] = moved[:, :width]
+            out_ref[:, (p * n + g) * G:(p * n + g + 1) * G] = part[g * width:(g + 1) * width]
 
 
 def solution(mesh):
@@ -366,7 +367,7 @@
         layers = CYC_A + CYC_B + CYC_C
         return pl.pallas_call(
             functools.partial(kernel, n, nb),
-            out_shape=jax.ShapeDtypeStruct((boundary.shape[1], G // n), F32),
+            out_shape=jax.ShapeDtypeStruct((G // n, boundary.shape[1]), F32),
             in_specs=[pl.BlockSpec(memory_space=pltpu.HBM)] * 3,
             out_specs=pl.BlockSpec(memory_space=pltpu.VMEM),
             scratch_shapes=[
@@ -397,9 +398,9 @@
                 pltpu.SemaphoreType.DMA((2,)),
             ],
             compiler_params=pltpu.CompilerParams(
-                collective_id=0, has_side_effects=True, vmem_limit_bytes=40 * 2**20
+                collective_id=0, has_side_effects=True, vmem_limit_bytes=VMEM_BYTES
             ),
-        )(boundary, gate_stack, coupling)
+        )(boundary, gate_stack, coupling).T
 
     return jax.shard_map(
         on_device, mesh=mesh, in_specs=(P("cuts", "bits", None), P(), P()), out_specs=P("bits", "cuts"), check_vma=False

time: 48.2 us -> 45.2 us (0.938)
  local copies, waits for them, and re-layouts: 5.02 us -> 1.67 us
    unnamed x6 -> x1, local copies, waits for them, and re-layouts: 4.01 us -> 1.67 us
    pallas_call x1 -> x0, local copies, waits for them, and re-layouts: 1.01 us -> none  [on_device(): pl.pallas_call(functools.partial(kernel, n, nb), out_shape=jax.ShapeDtype...]
where the time goes in v2:
time: 45.2 us; the launch traced here: 45.1 us
  Pallas kernels  43.4 us (96%)
  local copies, waits for them, and re-layouts  1.67 us (4%)
    pallas_call x1, Pallas kernels, on_device(): pl.pallas_call(functools.partial(kernel, n, nb), out_shape=jax.ShapeDtype...  43.4 us
    unnamed x1, local copies, waits for them, and re-layouts  1.67 us

profile of v2, /device:TPU:0, one launch (start us, length us, event | category | flops | bytes accessed | tf_op | source)
XLA Modules:
  0.0 45.1 jit_solution(7696018357986864812)
XLA Ops:
  0.0 43.4 %shard_map.37 = f32[32,2048]{1,0:T(8,128)} custom-call(f32[1,2048,128]{2,1,0:T(8,128)} %x_hbm.1, f32[34,128,128]{2,1,0:T(8,128)} %gate_hbm.1, f32[13,128,128]{2,1,0:T(8,128)} %cpl_hbm.1), custom_call_target="tpu_custom_call" | custom-call | tf_op jit(solution)/shard_map/pallas_call | solution.py:368
  43.4 1.7 %copy.5 = f32[2048,32]{0,1:T(8,128)} copy(f32[2048,32]{0,1:T(8,128)} %bitcast.1) | data formatting | bytes 524288

commit v3 on v2

--- a/solution.py
+++ b/solution.py
@@ -14,7 +14,8 @@
 G = 128
 F32 = jnp.float32
 BF16 = jnp.bfloat16
-VMEM_BYTES = 63 * 2**20 + 2**19
+SLAB = 16
+VMEM_BYTES = 63 * 2**20 + 2**18
 
 
 def split(x):
@@ -24,11 +25,11 @@
 
 
 def left_gate(w_ref, index, x):
-    hi, lo = w_ref[index, 0], w_ref[index, 1]
-    lhs = jnp.concatenate([jnp.concatenate([hi, hi], 1), jnp.concatenate([lo, lo], 1)], 0)
+    w = w_ref[index]
     xh, xl = split(x)
-    y = jnp.dot(lhs, jnp.concatenate([xh, xl], 0), preferred_element_type=F32)
-    return y[:G] + y[G:]
+    y = jnp.dot(jnp.concatenate([w, w], 1), jnp.concatenate([xh, xl], 0), preferred_element_type=F32)
+    y = y.reshape(G // SLAB, 2, SLAB, x.shape[1])
+    return (y[:, 0] + y[:, 1]).reshape(x.shape)
 
 
 def right_gate(w_ref, index, x):
@@ -104,11 +105,11 @@
     pl.semaphore_signal(barrier, inc=1, device_id=(mate_top, me), device_id_type=MESH)
     pl.semaphore_signal(barrier, inc=1, device_id=(mate_low, me), device_id_type=MESH)
 
-    rounds = max(8 // n, 1)
+    rounds = 2 * (8 // n) if n <= 8 else 1
 
     def share(ref, base, k, r):
         if n <= 8:
-            return ref.at[base + k * rounds + r]
+            return ref.at[base + k * (rounds // 2) + r // 2, pl.ds(r % 2 * 8, 8)]
         cut = n // 8
         return ref.at[base + k // cut, pl.ds((k % cut) * (16 // cut), 16 // cut)]
 
@@ -118,8 +119,8 @@
 
     def put(w_ref, index, value):
         hi, lo = split(value)
-        w_ref[index, 0] = hi
-        w_ref[index, 1] = lo
+        slabs = [part[i:i + SLAB] for i in range(0, G, SLAB) for part in (hi, lo)]
+        w_ref[index] = jnp.concatenate(slabs, 0)
 
     def reorder(load):
         return jnp.concatenate([load(c) for c in range(16)], 0)
@@ -128,7 +129,9 @@
         put(wt, index, (eye + 0.45 * gate_ref[gate]).T)
 
     def prep_lane(index, gate):
-        put(wl, index, eye + 0.45 * gate_ref[gate])
+        hi, lo = split(eye + 0.45 * gate_ref[gate])
+        wl[index, 0] = hi
+        wl[index, 1] = lo
 
     def prep_mid(index, gate, natural=False):
         rows = reorder(lambda c: gate_ref[gate, pl.ds(c, 8, stride=16), :])
@@ -173,10 +176,11 @@
         for j in range(0, len(blocks), 4):
             y = right_gate(wl, layer, jnp.concatenate([x[blocks[j + u]].reshape(G, G) for u in range(4)], 0))
             table = tab[layer]
-            y = jnp.concatenate([y[u * G:(u + 1) * G] * table for u in range(4)], 1)
-            y = left_gate(wm, layer, y)
-            for u in range(4):
-                x[blocks[j + u]] = y[:, u * G:(u + 1) * G].reshape(16, 8, G)
+            for v in (0, 2):
+                z = jnp.concatenate([y[u * G:(u + 1) * G] * table for u in (v, v + 1)], 1)
+                z = left_gate(wm, layer, z)
+                for u in range(2):
+                    x[blocks[j + v + u]] = z[:, u * G:(u + 1) * G].reshape(16, 8, G)
 
     loads[0].wait()
     prep_layers(0, 1)
@@ -198,8 +202,9 @@
 
     rs = []
     for r in range(rounds):
-        if rounds == 2:
-            lane_mid(CYC_A - 1, [out_base + 2 * i + r for i in range(4)])
+        if rounds == 4:
+            if r % 2 == 0:
+                lane_mid(CYC_A - 1, [out_base + 2 * i + r // 2 for i in range(4)])
         elif r == 0:
             lane_mid(CYC_A - 1, [out_base + i for i in range(8)])
         if r == 0:
@@ -358,8 +363,8 @@
 def solution(mesh):
     n, nb = mesh.shape["cuts"], mesh.shape["bits"]
     groups = 16 // n
-    rounds = max(8 // n, 1)
-    part = (rounds, 16 // max(n // 8, 1), 8, G)
+    rounds = 2 * (8 // n) if n <= 8 else 1
+    part = (rounds, 8 if n <= 8 else 16 // (n // 8), 8, G)
     messages = 3 * groups if n == 4 else n - 1
 
     def on_device(boundary, gate_stack, coupling):
@@ -375,9 +380,9 @@
                 pltpu.VMEM((gates, G, G), F32),
                 pltpu.VMEM((tables, G, G), F32),
                 pltpu.VMEM((16, 16, 8, G), F32),
-                pltpu.VMEM((layers, 2, G, G), BF16),
+                pltpu.VMEM((layers, 2 * G, G), BF16),
                 pltpu.VMEM((CYC_A + CYC_B, 2, G, G), BF16),
-                pltpu.VMEM((layers, 2, G, G), BF16),
+                pltpu.VMEM((layers, 2 * G, G), BF16),
                 pltpu.VMEM((layers, G, G), F32),
                 pltpu.VMEM((G, G), F32),
                 pltpu.VMEM((rounds, n - 1) + part[1:], F32),

time: 45.2 us -> 44.8 us (level)
  Pallas kernels: 43.4 us -> 42.9 us
    pallas_call x1, Pallas kernels: 43.4 us -> 42.9 us  [on_device(): pl.pallas_call(functools.partial(kernel, n, nb), out_shape=jax.ShapeDtype...]
where the time goes in v3:
time: 44.8 us; the launch traced here: 44.6 us
  Pallas kernels  42.9 us (96%)
  local copies, waits for them, and re-layouts  1.67 us (4%)
    pallas_call x1, Pallas kernels, on_device(): pl.pallas_call(functools.partial(kernel, n, nb), out_shape=jax.ShapeDtype...  42.9 us
    unnamed x1, local copies, waits for them, and re-layouts  1.67 us

profile of v3, /device:TPU:0, one launch (start us, length us, event | category | flops | bytes accessed | tf_op | source)
XLA Modules:
  0.0 44.6 jit_solution(6599296069775499512)
XLA Ops:
  0.0 42.9 %shard_map.37 = f32[32,2048]{1,0:T(8,128)} custom-call(f32[1,2048,128]{2,1,0:T(8,128)} %x_hbm.1, f32[34,128,128]{2,1,0:T(8,128)} %gate_hbm.1, f32[13,128,128]{2,1,0:T(8,128)} %cpl_hbm.1), custom_call_target="tpu_custom_call" | custom-call | tf_op jit(solution)/shard_map/pallas_call | solution.py:373
  43.0 1.7 %copy.5 = f32[2048,32]{0,1:T(8,128)} copy(f32[2048,32]{0,1:T(8,128)} %bitcast.1) | data formatting | bytes 524288

commit v4 on v3

--- a/solution.py
+++ b/solution.py
@@ -15,7 +15,7 @@
 F32 = jnp.float32
 BF16 = jnp.bfloat16
 SLAB = 16
-VMEM_BYTES = 63 * 2**20 + 2**18
+VMEM_BYTES = 63 * 2**20
 
 
 def split(x):
@@ -83,9 +83,6 @@
     load_x = pltpu.make_async_copy(x_hbm.at[0], x_in, in_sem.at[4])
     loads[0].start()
     load_x.start()
-    load_cpl.start()
-    loads[1].start()
-    loads[2].start()
 
     me = lax.axis_index("cuts")
     bit = lax.axis_index("bits")
@@ -166,29 +163,30 @@
         pl.loop(first, first + count)(prep_layer)
 
     def top(layer):
-        for j in range(8):
-            pair = [x[:, 2 * j + u].reshape(G, G) for u in range(2)]
-            y = left_gate(wt, layer, jnp.concatenate(pair, 1))
-            for u in range(2):
-                x[:, 2 * j + u] = y[:, u * G:(u + 1) * G].reshape(16, 8, G)
+        for j in range(0, 16, 4):
+            y = left_gate(wt, layer, jnp.concatenate([x[:, j + u].reshape(G, G) for u in range(4)], 1))
+            for u in range(4):
+                x[:, j + u] = y[:, u * G:(u + 1) * G].reshape(16, 8, G)
 
     def lane_mid(layer, blocks):
         for j in range(0, len(blocks), 4):
             y = right_gate(wl, layer, jnp.concatenate([x[blocks[j + u]].reshape(G, G) for u in range(4)], 0))
             table = tab[layer]
-            for v in (0, 2):
-                z = jnp.concatenate([y[u * G:(u + 1) * G] * table for u in (v, v + 1)], 1)
-                z = left_gate(wm, layer, z)
-                for u in range(2):
-                    x[blocks[j + v + u]] = z[:, u * G:(u + 1) * G].reshape(16, 8, G)
+            y = jnp.concatenate([y[u * G:(u + 1) * G] * table for u in range(4)], 1)
+            y = left_gate(wm, layer, y)
+            for u in range(4):
+                x[blocks[j + u]] = y[:, u * G:(u + 1) * G].reshape(16, 8, G)
 
     loads[0].wait()
     prep_layers(0, 1)
+    load_x.wait()
+    load_cpl.start()
+    loads[1].start()
+    loads[2].start()
+    for t in range(16):
+        x[:, t] = x_in[pl.ds(t, G, stride=16), :].reshape(16, 8, G)
     load_cpl.wait()
     prep_table(0, False)
-    load_x.wait()
-    for t in range(16):
-        x[:, t] = x_in[pl.ds(t, G, stride=16), :].reshape(16, 8, G)
     loads[1].wait()
 
     @pl.loop(0, CYC_A - 1)
@@ -272,11 +270,6 @@
 
     final = CYC_A + CYC_B - 1
     top(final)
-    for p in range(groups):
-        y = right_gate(wl, final, x[pl.ds(p * n, n)].reshape(n * G, G))
-        parts = transpose_blocks([y[g * G:(g + 1) * G] for g in range(n)], width)
-        for k in range(n):
-            sbuf[k, p] = parts[k].reshape(16, 8, G)
 
     def send(src, dst, index, to):
         copy = pltpu.make_async_remote_copy(
@@ -286,29 +279,33 @@
         copy.start()
         return copy
 
-    fin = []
+    near = (me + 1 - 2 * (me % 2), me + 2 - 4 * (me // 2))
+    far = 3 - me
+    first, second, third = [], [], []
+    for p in range(groups):
+        y = right_gate(wl, final, x[pl.ds(p * n, n)].reshape(n * G, G))
+        parts = transpose_blocks([y[g * G:(g + 1) * G] for g in range(n)], width)
+        for k in range(n):
+            sbuf[k, p] = parts[k].reshape(16, 8, G)
+        if n == 4:
+            first.append(send(sbuf.at[far, p], rbuf.at[0, p], p, near[p % 2]))
     if n == 4:
-        near = (me + 1 - 2 * (me % 2), me + 2 - 4 * (me // 2))
-        far = 3 - me
-        first = [send(sbuf.at[far, p], rbuf.at[0, p], p, near[p % 2]) for p in range(groups)]
-        second = [send(sbuf.at[near[p % 2], p], rbuf.at[1, p], groups + p, near[p % 2]) for p in range(groups)]
-        third = []
+        for p in range(groups):
+            second.append(send(sbuf.at[near[p % 2], p], rbuf.at[1, p], groups + p, near[p % 2]))
         for p in range(groups):
             first[p].wait_recv()
             to = near[1 - p % 2]
             sbuf[to, p] = sbuf[to, p] + rbuf[0, p]
             third.append(send(sbuf.at[to, p], rbuf.at[2, p], 2 * groups + p, to))
-        for copy in second + third:
-            copy.wait_recv()
-        fin = first + second + third
         terms = (1, 2)
     else:
         for d in range(1, n):
             to = lax.rem(me + d, n)
-            fin.append(send(sbuf.at[to], rbuf.at[d - 1], d - 1, to))
-        for copy in fin:
-            copy.wait_recv()
+            second.append(send(sbuf.at[to], rbuf.at[d - 1], d - 1, to))
         terms = range(n - 1)
+    for copy in second + third:
+        copy.wait_recv()
+    fin = first + second + third
 
     def mid_packed(layer, load):
         table = tab[layer]

time: 44.8 us -> 45.5 us (1.016)
  Pallas kernels: 42.9 us -> 43.6 us
    pallas_call x1, Pallas kernels: 42.9 us -> 43.6 us  [on_device(): pl.pallas_call(functools.partial(kernel, n, nb), out_shape=jax.ShapeDtype...]
where the time goes in v4:
time: 45.5 us; the launch traced here: 45.3 us
  Pallas kernels  43.6 us (96%)
  local copies, waits for them, and re-layouts  1.67 us (4%)
    pallas_call x1, Pallas kernels, on_device(): pl.pallas_call(functools.partial(kernel, n, nb), out_shape=jax.ShapeDtype...  43.6 us
    unnamed x1, local copies, waits for them, and re-layouts  1.67 us

profile of v4, /device:TPU:0, one launch (start us, length us, event | category | flops | bytes accessed | tf_op | source)
XLA Modules:
  0.0 45.3 jit_solution(15135081474762523239)
XLA Ops:
  0.0 43.6 %shard_map.37 = f32[32,2048]{1,0:T(8,128)} custom-call(f32[1,2048,128]{2,1,0:T(8,128)} %x_hbm.1, f32[34,128,128]{2,1,0:T(8,128)} %gate_hbm.1, f32[13,128,128]{2,1,0:T(8,128)} %cpl_hbm.1), custom_call_target="tpu_custom_call" | custom-call | tf_op jit(solution)/shard_map/pallas_call | solution.py:370
  43.6 1.7 %copy.5 = f32[2048,32]{0,1:T(8,128)} copy(f32[2048,32]{0,1:T(8,128)} %bitcast.1) | data formatting | bytes 524288

commit v5 on v4

--- a/solution.py
+++ b/solution.py
@@ -74,7 +74,7 @@
     x_in, gate_ref, cpl_ref, x, wt, wl, wm, tab, tmp, rs_buf, red, swp, sbuf, rbuf, mp, tp, in0,
     in_sem, rs_send, rs_recv, swp_send, swp_recv, fin_send, fin_recv, in0_sem,
 ):
-    spans = ((0, 3), (3, 3 * CYC_A), (3 * CYC_A, gate_ref.shape[0]))
+    spans = ((0, 4), (4, 3 * CYC_A + 1), (3 * CYC_A + 1, gate_ref.shape[0]))
     loads = [
         pltpu.make_async_copy(gate_hbm.at[pl.ds(a, b - a)], gate_ref.at[pl.ds(a, b - a)], in_sem.at[i])
         for i, (a, b) in enumerate(spans)
@@ -162,41 +162,43 @@
     def prep_layers(first, count):
         pl.loop(first, first + count)(prep_layer)
 
-    def top(layer):
-        for j in range(0, 16, 4):
-            y = left_gate(wt, layer, jnp.concatenate([x[:, j + u].reshape(G, G) for u in range(4)], 1))
-            for u in range(4):
+    def top(layer, load=lambda t: x[:, t].reshape(G, G)):
+        for j in range(0, 16, 2):
+            y = left_gate(wt, layer, jnp.concatenate([load(j), load(j + 1)], 1))
+            for u in range(2):
                 x[:, j + u] = y[:, u * G:(u + 1) * G].reshape(16, 8, G)
 
     def lane_mid(layer, blocks):
-        for j in range(0, len(blocks), 4):
-            y = right_gate(wl, layer, jnp.concatenate([x[blocks[j + u]].reshape(G, G) for u in range(4)], 0))
-            table = tab[layer]
-            y = jnp.concatenate([y[u * G:(u + 1) * G] * table for u in range(4)], 1)
+        table = tab[layer]
+        for j in range(0, len(blocks), 2):
+            y = right_gate(wl, layer, jnp.concatenate([x[blocks[j + u]].reshape(G, G) for u in range(2)], 0))
+            y = jnp.concatenate([y[u * G:(u + 1) * G] * table for u in range(2)], 1)
             y = left_gate(wm, layer, y)
-            for u in range(4):
+            for u in range(2):
                 x[blocks[j + u]] = y[:, u * G:(u + 1) * G].reshape(16, 8, G)
 
     loads[0].wait()
-    prep_layers(0, 1)
+    prep_top(0, 0)
     load_x.wait()
     load_cpl.start()
     loads[1].start()
     loads[2].start()
-    for t in range(16):
-        x[:, t] = x_in[pl.ds(t, G, stride=16), :].reshape(16, 8, G)
+    top(0, lambda t: x_in[pl.ds(t, G, stride=16), :])
+    prep_lane(0, 1)
+    prep_mid(0, 2)
+    prep_top(1, 3)
     load_cpl.wait()
     prep_table(0, False)
     loads[1].wait()
 
     @pl.loop(0, CYC_A - 1)
     def _(layer):
-        top(layer)
         lane_mid(layer, range(16))
-        prep_layer(layer + 1)
+        top(layer + 1)
+        prep_lane(layer + 1, 3 * layer + 4)
+        prep_mid(layer + 1, 3 * layer + 5)
+        prep_top(layer + 2, 3 * layer + 6)
         prep_table(layer + 1, False)
-
-    top(CYC_A - 1)
 
     rs = []
     for r in range(rounds):
@@ -263,13 +265,14 @@
         swaps[r].wait()
         share(x, out_base, me, r)[...] = swp[r]
 
+    top(CYC_A)
+
     @pl.loop(CYC_A, CYC_A + CYC_B - 1)
     def _(layer):
-        top(layer)
         lane_mid(layer, range(16))
+        top(layer + 1)
 
     final = CYC_A + CYC_B - 1
-    top(final)
 
     def send(src, dst, index, to):
         copy = pltpu.make_async_remote_copy(

time: 45.5 us -> 45.5 us (level)
  no operation moved by 1% of the time
where the time goes in v5:
time: 45.5 us; the launch traced here: 45.3 us
  Pallas kernels  43.6 us (96%)
  local copies, waits for them, and re-layouts  1.67 us (4%)
    pallas_call x1, Pallas kernels, on_device(): pl.pallas_call(functools.partial(kernel, n, nb), out_shape=jax.ShapeDtype...  43.6 us
    unnamed x1, local copies, waits for them, and re-layouts  1.67 us

profile of v5, /device:TPU:0, one launch (start us, length us, event | category | flops | bytes accessed | tf_op | source)
XLA Modules:
  0.0 45.3 jit_solution(3544930104363651059)
XLA Ops:
  0.0 43.6 %shard_map.37 = f32[32,2048]{1,0:T(8,128)} custom-call(f32[1,2048,128]{2,1,0:T(8,128)} %x_hbm.1, f32[34,128,128]{2,1,0:T(8,128)} %gate_hbm.1, f32[13,128,128]{2,1,0:T(8,128)} %cpl_hbm.1), custom_call_target="tpu_custom_call" | custom-call | tf_op jit(solution)/shard_map/pallas_call | solution.py:373
  43.6 1.7 %copy.5 = f32[2048,32]{0,1:T(8,128)} copy(f32[2048,32]{0,1:T(8,128)} %bitcast.1) | data formatting | bytes 524288

commit v6 on v5

--- a/solution.py
+++ b/solution.py
@@ -14,7 +14,6 @@
 G = 128
 F32 = jnp.float32
 BF16 = jnp.bfloat16
-SLAB = 16
 VMEM_BYTES = 63 * 2**20
 
 
@@ -25,11 +24,11 @@
 
 
 def left_gate(w_ref, index, x):
-    w = w_ref[index]
+    hi, lo = w_ref[index, 0], w_ref[index, 1]
     xh, xl = split(x)
-    y = jnp.dot(jnp.concatenate([w, w], 1), jnp.concatenate([xh, xl], 0), preferred_element_type=F32)
-    y = y.reshape(G // SLAB, 2, SLAB, x.shape[1])
-    return (y[:, 0] + y[:, 1]).reshape(x.shape)
+    return jnp.dot(
+        jnp.concatenate([hi, hi, lo], 1), jnp.concatenate([xh, xl, xh], 0), preferred_element_type=F32
+    )
 
 
 def right_gate(w_ref, index, x):
@@ -83,6 +82,8 @@
     load_x = pltpu.make_async_copy(x_hbm.at[0], x_in, in_sem.at[4])
     loads[0].start()
     load_x.start()
+    loads[1].start()
+    load_cpl.start()
 
     me = lax.axis_index("cuts")
     bit = lax.axis_index("bits")
@@ -116,8 +117,8 @@
 
     def put(w_ref, index, value):
         hi, lo = split(value)
-        slabs = [part[i:i + SLAB] for i in range(0, G, SLAB) for part in (hi, lo)]
-        w_ref[index] = jnp.concatenate(slabs, 0)
+        w_ref[index, 0] = hi
+        w_ref[index, 1] = lo
 
     def reorder(load):
         return jnp.concatenate([load(c) for c in range(16)], 0)
@@ -126,9 +127,7 @@
         put(wt, index, (eye + 0.45 * gate_ref[gate]).T)
 
     def prep_lane(index, gate):
-        hi, lo = split(eye + 0.45 * gate_ref[gate])
-        wl[index, 0] = hi
-        wl[index, 1] = lo
+        put(wl, index, eye + 0.45 * gate_ref[gate])
 
     def prep_mid(index, gate, natural=False):
         rows = reorder(lambda c: gate_ref[gate, pl.ds(c, 8, stride=16), :])
@@ -180,8 +179,6 @@
     loads[0].wait()
     prep_top(0, 0)
     load_x.wait()
-    load_cpl.start()
-    loads[1].start()
     loads[2].start()
     top(0, lambda t: x_in[pl.ds(t, G, stride=16), :])
     prep_lane(0, 1)
@@ -380,9 +377,9 @@
                 pltpu.VMEM((gates, G, G), F32),
                 pltpu.VMEM((tables, G, G), F32),
                 pltpu.VMEM((16, 16, 8, G), F32),
-                pltpu.VMEM((layers, 2 * G, G), BF16),
+                pltpu.VMEM((layers, 2, G, G), BF16),
                 pltpu.VMEM((CYC_A + CYC_B, 2, G, G), BF16),
-                pltpu.VMEM((layers, 2 * G, G), BF16),
+                pltpu.VMEM((layers, 2, G, G), BF16),
                 pltpu.VMEM((layers, G, G), F32),
                 pltpu.VMEM((G, G), F32),
                 pltpu.VMEM((rounds, n - 1) + part[1:], F32),

time: 45.5 us -> 43.4 us (0.954)
  Pallas kernels: 43.6 us -> 41.5 us
    pallas_call x1, Pallas kernels: 43.6 us -> 41.5 us  [on_device(): pl.pallas_call(functools.partial(kernel, n, nb), out_shape=jax.ShapeDtype...]
where the time goes in v6:
time: 43.4 us; the launch traced here: 43.2 us
  Pallas kernels  41.5 us (96%)
  local copies, waits for them, and re-layouts  1.67 us (4%)
    pallas_call x1, Pallas kernels, on_device(): pl.pallas_call(functools.partial(kernel, n, nb), out_shape=jax.ShapeDtype...  41.5 us
    unnamed x1, local copies, waits for them, and re-layouts  1.67 us

profile of v6, /device:TPU:0, one launch (start us, length us, event | category | flops | bytes accessed | tf_op | source)
XLA Modules:
  0.0 43.2 jit_solution(2923388856873465252)
XLA Ops:
  0.0 41.5 %shard_map.37 = f32[32,2048]{1,0:T(8,128)} custom-call(f32[1,2048,128]{2,1,0:T(8,128)} %x_hbm.1, f32[34,128,128]{2,1,0:T(8,128)} %gate_hbm.1, f32[13,128,128]{2,1,0:T(8,128)} %cpl_hbm.1), custom_call_target="tpu_custom_call" | custom-call | tf_op jit(solution)/shard_map/pallas_call | solution.py:370
  41.6 1.7 %copy.5 = f32[2048,32]{0,1:T(8,128)} copy(f32[2048,32]{0,1:T(8,128)} %bitcast.1) | data formatting | bytes 524288

commit v7 on v6

--- a/solution.py
+++ b/solution.py
@@ -162,10 +162,12 @@
         pl.loop(first, first + count)(prep_layer)
 
     def top(layer, load=lambda t: x[:, t].reshape(G, G)):
-        for j in range(0, 16, 2):
-            y = left_gate(wt, layer, jnp.concatenate([load(j), load(j + 1)], 1))
-            for u in range(2):
-                x[:, j + u] = y[:, u * G:(u + 1) * G].reshape(16, 8, G)
+        @pl.loop(0, 4)
+        def _(step):
+            for j in (4 * step, 4 * step + 2):
+                y = left_gate(wt, layer, jnp.concatenate([load(j), load(j + 1)], 1))
+                for u in range(2):
+                    x[:, j + u] = y[:, u * G:(u + 1) * G].reshape(16, 8, G)
 
     def lane_mid(layer, blocks):
         table = tab[layer]
@@ -188,9 +190,14 @@
     prep_table(0, False)
     loads[1].wait()
 
+    def lane_mid_run(layer, base, count):
+        @pl.loop(0, count // 4)
+        def _(step):
+            lane_mid(layer, [base + 4 * step + u for u in range(4)])
+
     @pl.loop(0, CYC_A - 1)
     def _(layer):
-        lane_mid(layer, range(16))
+        lane_mid_run(layer, 0, 16)
         top(layer + 1)
         prep_lane(layer + 1, 3 * layer + 4)
         prep_mid(layer + 1, 3 * layer + 5)
@@ -215,7 +222,7 @@
                 device_id=(bit, to), device_id_type=MESH,
             ))
             rs[r][-1].start()
-    lane_mid(CYC_A - 1, [stay_base + i for i in range(8)])
+    lane_mid_run(CYC_A - 1, stay_base, 8)
     loads[2].wait()
 
     swaps = []
@@ -266,7 +273,7 @@
 
     @pl.loop(CYC_A, CYC_A + CYC_B - 1)
     def _(layer):
-        lane_mid(layer, range(16))
+        lane_mid_run(layer, 0, 16)
         top(layer + 1)
 
     final = CYC_A + CYC_B - 1

time: 43.4 us -> 54.4 us (1.25)
  Pallas kernels: 41.5 us -> 52.6 us
    pallas_call x1, Pallas kernels: 41.5 us -> 52.6 us  [on_device(): pl.pallas_call(functools.partial(kernel, n, nb), out_shape=jax.ShapeDtype...]
where the time goes in v7:
time: 54.4 us; the launch traced here: 54.2 us
  Pallas kernels  52.6 us (97%)
  local copies, waits for them, and re-layouts  1.67 us (3%)
    pallas_call x1, Pallas kernels, on_device(): pl.pallas_call(functools.partial(kernel, n, nb), out_shape=jax.ShapeDtype...  52.6 us
    unnamed x1, local copies, waits for them, and re-layouts  1.67 us

profile of v7, /device:TPU:0, one launch (start us, length us, event | category | flops | bytes accessed | tf_op | source)
XLA Modules:
  0.0 54.2 jit_solution(4056416124047656502)
XLA Ops:
  0.0 52.6 %shard_map.37 = f32[32,2048]{1,0:T(8,128)} custom-call(f32[1,2048,128]{2,1,0:T(8,128)} %x_hbm.1, f32[34,128,128]{2,1,0:T(8,128)} %gate_hbm.1, f32[13,128,128]{2,1,0:T(8,128)} %cpl_hbm.1), custom_call_target="tpu_custom_call" | custom-call | tf_op jit(solution)/shard_map/pallas_call | solution.py:377
  52.6 1.7 %copy.5 = f32[2048,32]{0,1:T(8,128)} copy(f32[2048,32]{0,1:T(8,128)} %bitcast.1) | data formatting | bytes 524288

commit v8 on v6

--- a/solution.py
+++ b/solution.py
@@ -188,8 +188,7 @@
     prep_table(0, False)
     loads[1].wait()
 
-    @pl.loop(0, CYC_A - 1)
-    def _(layer):
+    for layer in range(CYC_A - 1):
         lane_mid(layer, range(16))
         top(layer + 1)
         prep_lane(layer + 1, 3 * layer + 4)
@@ -264,8 +263,7 @@
 
     top(CYC_A)
 
-    @pl.loop(CYC_A, CYC_A + CYC_B - 1)
-    def _(layer):
+    for layer in range(CYC_A, CYC_A + CYC_B - 1):
         lane_mid(layer, range(16))
         top(layer + 1)
 
@@ -341,8 +339,7 @@
         put_packed(tp, left_gate(wt, layer, y))
         repack(tp, mp, n, width)
 
-    @pl.loop(last, last + CYC_C - 1)
-    def _(layer):
+    for layer in range(last, last + CYC_C - 1):
         top_packed(layer)
         put_packed(mp, mid_packed(layer, lambda p: mp[p].reshape(G, G)))
         repack(mp, tp, n, width)

time: 43.4 us -> 42.5 us (0.979)
  Pallas kernels: 41.5 us -> 40.6 us
    pallas_call x1, Pallas kernels: 41.5 us -> 40.6 us  [on_device(): pl.pallas_call(functools.partial(kernel, n, nb), out_shape=jax.ShapeDtype...]
where the time goes in v8:
time: 42.5 us; the launch traced here: 42.3 us
  Pallas kernels  40.6 us (96%)
  local copies, waits for them, and re-layouts  1.67 us (4%)
    pallas_call x1, Pallas kernels, on_device(): pl.pallas_call(functools.partial(kernel, n, nb), out_shape=jax.ShapeDtype...  40.6 us
    unnamed x1, local copies, waits for them, and re-layouts  1.67 us

profile of v8, /device:TPU:0, one launch (start us, length us, event | category | flops | bytes accessed | tf_op | source)
XLA Modules:
  0.0 42.3 jit_solution(15457700835438476297)
XLA Ops:
  0.0 40.6 %shard_map.37 = f32[32,2048]{1,0:T(8,128)} custom-call(f32[1,2048,128]{2,1,0:T(8,128)} %x_hbm.1, f32[34,128,128]{2,1,0:T(8,128)} %gate_hbm.1, f32[13,128,128]{2,1,0:T(8,128)} %cpl_hbm.1), custom_call_target="tpu_custom_call" | custom-call | tf_op jit(solution)/shard_map/pallas_call | solution.py:367
  40.6 1.7 %copy.5 = f32[2048,32]{0,1:T(8,128)} copy(f32[2048,32]{0,1:T(8,128)} %bitcast.1) | data formatting | bytes 524288
